TPU v7x, 128 devices: a whole 4x4x4 slice. The times are simulated.
128 devices in a mesh: blk: 16 (over z, x_hi, core), group: 8 (over y, x_lo).
Axes of the slice: x: 4 (x_hi: 2, x_lo: 2; x = x_hi * 2 + x_lo), y: 4, z: 4, core: 2. Of those that a mesh axis runs over, the one named last changes fastest.
Arguments:
- images: bfloat16 [22528, 1152], P(('blk', 'group')), may hold values from -0.1796875 to 0.1796875
- texts: bfloat16 [22528, 1152], P(('blk', 'group')), may hold values from -0.1796875 to 0.1796875
- match: int32 [22528], P(('blk', 'group')), may hold values from 0 to 22527, each once
- logit_scale: float32 [1], replicated, may hold values from 20 to 40
- logit_bias: float32 [1], replicated, may hold values from -7 to -4
Outputs:
- image_grad: float32 [22528, 1152], P(('blk', 'group'))
- text_grad: float32 [22528, 1152], P(('blk', 'group'))
Inputs may be any that keep to these rules, and one draw needn't show every extreme that they name: match holds each text index exactly once.
All inputs are finite; a program needn't handle non-finite values.
Results may differ from a plain program's by a relative error of at most 0.008.
Values may be sent and summed in bfloat16 or wider, within the bound.
A program may use at most 128 MiB of HBM per device.

v0:
```python
import jax
import jax.numpy as jnp
from jax import lax
from jax.experimental import pallas as pl
from jax.experimental.pallas import tpu as pltpu
from jax.sharding import PartitionSpec as P

epsilon = 1e-06
MESH = pl.DeviceIdType.MESH
ROWS, WIDTH = 176, 1152
EARLY, LATE = 96, 80
FIRST, LAST = 64, 48
IMAGES, TEXTS = 8 * ROWS, 16 * ROWS
SEMS = 208
bf16, f32 = jnp.bfloat16, jnp.float32


def place():
    b, g = lax.axis_index("blk"), lax.axis_index("group")
    x = lax.rem(b // 2, 2) * 2 + lax.rem(g, 2)
    return x, g // 2, b // 4, lax.rem(b, 2)


def device(x, y, z, core):
    return ((z * 2 + x // 2) * 2 + core, y * 2 + lax.rem(x, 2))


def unit_rows(x):
    values = x.astype(f32)
    scale = lax.rsqrt(jnp.sum(values * values, axis=1, keepdims=True) + epsilon)
    return values * scale, scale


def norm_back(x, grad):
    unit, scale = unit_rows(x)
    inner = jnp.sum(unit * grad, axis=1, keepdims=True)
    return scale * (grad - unit * inner)


class Links:
    def __init__(self, send_sems, recv_sems):
        self.send_sems, self.recv_sems = send_sems, recv_sems
        self.copies, self.started, self.sent = {}, [], 0

    def plan(self, name, src, dst, target):
        self.copies[name] = len(self.copies), src, dst, target

    def copy(self, name):
        k, src, dst, target = self.copies[name]
        return pltpu.make_async_remote_copy(
            src_ref=src(), dst_ref=dst(), send_sem=self.send_sems.at[k], recv_sem=self.recv_sems.at[k],
            device_id=target, device_id_type=MESH,
        )

    def start(self, name):
        self.copy(name).start()
        self.started.append(name)

    def send(self, name, src, dst, target):
        self.plan(name, src, dst, target)
        self.start(name)

    def arrived(self, *names):
        for name in names:
            self.copy(name).wait_recv()

    def finish(self):
        for name in self.started[self.sent :]:
            self.copy(name).wait_send()
        self.sent = len(self.started)


class Part:
    def __init__(self, tag, links, ways, slots, sums, base, first, rows, cut, half_a, half_b, inbox, box):
        self.tag, self.links = tag, links
        self.up, self.down, self.partner = ways
        self.slots, self.sums, self.base, self.first, self.rows = slots, sums, base, first, rows
        self.all, self.a, self.b = (0, rows), (0, cut), (cut, rows)
        self.a0, self.a1, self.b0, self.b1 = (0, half_a), (half_a, cut), (cut, half_b), (half_b, rows)
        self.inbox, self.box, self.boxes, self.empty = inbox, box, {}, set()

    def span(self, r, p, part):
        return pl.ds(self.base + (r * 2 + p) * self.rows + part[0], part[1] - part[0])

    def at(self, r, p, part):
        return lambda: self.slots.at[self.span(r, p, part)]

    def plan(self, name, part, src, dst, target):
        if part[1] > part[0]:
            self.links.plan(self.tag + name, src, dst, target)
        else:
            self.empty.add(name)

    def give(self, *names):
        for name in names:
            if name not in self.empty:
                self.links.start(self.tag + name)

    def arrived(self, *names):
        self.links.arrived(*(self.tag + n for n in names if n not in self.empty))

    def plan_gather(self):
        up, down, partner, a, b = self.up, self.down, self.partner, self.a, self.b
        moves = [("gB", 0, 0, 0, 1, b, partner), ("gA", 0, 0, 0, 1, a, partner)]
        moves += [(f"gD{r}", r, 0, r, 1, a, partner) for r in (1, 2, 3)]
        for name, p, part in (("gA", 0, a), ("gB", 0, b), ("gC", 1, b)):
            moves += [(name + "3", 0, p, 3, p, part, up), (name + "1", 0, p, 1, p, part, down)]
            half0, half1 = (self.a0, self.a1) if part is a else (self.b0, self.b1)
            moves += [(name + "20", 1, p, 2, p, half0, down), (name + "21", 3, p, 2, p, half1, up)]
        for name, r, p, to_r, to_p, part, target in moves:
            self.plan(name, part, self.at(r, p, part), self.at(to_r, to_p, part), target)

    def gather_start(self):
        self.give("gB", "gA3", "gA1", "gB3", "gB1", "gA")

    def gather_pair(self):
        self.arrived("gB")
        self.give("gC3", "gC1")

    def gather_a(self):
        self.arrived("gA1", "gA3")
        self.give("gA20", "gA21", "gD1", "gD3")

    def gather_b(self):
        self.arrived("gB1", "gB3")
        self.give("gB20", "gB21")

    def gather_a2(self):
        self.arrived("gA20", "gA21")
        self.give("gD2")

    def gather_c(self):
        self.arrived("gC1", "gC3")
        self.give("gC20", "gC21")

    def plan_sums(self):
        up, down = self.up, self.down
        moves = [(f"sX{r}", r, 1, self.a, self.partner) for r in range(4)] + [("sXB", 0, 1, self.b, self.partner)]
        moves += [("sHA1", 2, 0, self.a0, up), ("sHA3", 2, 0, self.a1, down)]
        moves += [("sRA1", 1, 0, self.a, up), ("sRA3", 3, 0, self.a, down)]
        for p in (0, 1):
            moves += [(f"sH1{p}", 2, p, self.b0, up), (f"sH3{p}", 2, p, self.b1, down)]
            moves += [(f"sR1{p}", 1, p, self.b, up), (f"sR3{p}", 3, p, self.b, down)]
        for name, r, p, part, target in moves:
            src, size = self.span(r, p, part), part[1] - part[0]
            dst = self.boxes[name] = pl.ds(self.box, size)
            self.box += size
            self.plan(name, part, lambda src=src: self.sums.at[src], lambda dst=dst: self.inbox.at[dst], target)

    def got(self, name):
        self.arrived(name)
        return self.inbox[self.boxes[name], :].astype(f32)

    def add(self, r, p, part, *names):
        if part[1] == part[0]:
            return
        where = self.span(r, p, part)
        total = self.sums[where, :].astype(f32)
        for name in names:
            total = total + self.got(name)
        self.sums[where, :] = total.astype(bf16)

    def sum_far(self):
        self.give("sX2", "sH11", "sH31", "sH10", "sH30")

    def sum_far_a(self):
        self.add(2, 0, self.a, "sX2")
        self.give("sHA1", "sHA3")

    def sum_pair(self, r):
        self.give(f"sX{r}")

    def sum_near(self, r):
        half = self.b0 if r == 1 else self.b1
        for p in (1, 0):
            self.add(r, p, half, f"sH{r}{p}")
            self.give(f"sR{r}{p}")

    def sum_near_a(self, r):
        half = self.a0 if r == 1 else self.a1
        self.add(r, 0, self.a, f"sX{r}")
        self.add(r, 0, half, f"sHA{r}")
        self.give(f"sRA{r}")

    def sum_own_b(self):
        self.add(0, 1, self.b, "sR11", "sR31")
        self.give("sXB")

    def total(self, own):
        top = self.got("sX0") + self.got("sRA1") + self.got("sRA3")
        bottom = self.got("sR10") + self.got("sR30") + self.got("sXB")
        return own + jnp.concatenate([top, bottom], axis=0)


def floor_div(a, n):
    return ((a.astype(f32) + 0.5) * (1.0 / n)).astype(jnp.int32)


def dot(a, b, ca, cb):
    return lax.dot_general(a, b, (((ca,), (cb,)), ((), ())), preferred_element_type=f32)


def kernel(
    images, texts, matches, scale_ref, bias_ref, image_grad, text_grad,
    i_slots, t_slots, m_slots, where_ref, w_ref, di, dt, t_own, t_sib, i_sums, i_inbox, t_inbox, send_sems, recv_sems,
):
    x, y, z, core = place()
    odd = lax.rem(x, 2)
    xi = x + 1 - 2 * odd
    xt = lax.rem(x + 3 + 2 * odd, 4)
    y_up, y_down, y_far = lax.rem(y + 1, 4), lax.rem(y + 3, 4), lax.rem(y + 2, 4)
    z_up, z_down = lax.rem(z + 1, 4), lax.rem(z + 3, 4)
    sibling = device(x, y, z, 1 - core)
    peers = {(r, p): device((x, xi)[p], (y, y_up, y_far, y_down)[r], z, core) for r in range(4) for p in range(2)}
    t_ways = device(x, y, z_up, core), device(x, y, z_down, core), device(xt, y, z, core)
    i_ways = peers[1, 0], peers[3, 0], peers[0, 1]

    barrier = pltpu.get_barrier_semaphore()
    greeted = [d for k, d in peers.items() if k != (0, 0)] + [*t_ways, sibling]
    for d in greeted:
        pl.semaphore_signal(barrier, inc=1, device_id=d, device_id_type=MESH)
    unit = unit_rows(images[...])[0].astype(bf16)
    i_slots[pl.ds(0, EARLY), :] = unit[:EARLY]
    i_slots[pl.ds(8 * EARLY, LATE), :] = unit[EARLY:]
    unit = unit_rows(texts[...])[0].astype(bf16)
    t_slots[pl.ds(0, FIRST), :] = unit[:FIRST]
    t_slots[pl.ds(16 * FIRST, FIRST), :] = unit[FIRST : 2 * FIRST]
    t_slots[pl.ds(32 * FIRST, LAST), :] = unit[2 * FIRST :]
    pl.semaphore_wait(barrier, len(greeted))

    links = Links(send_sems, recv_sems)
    Y = Part("Y", links, i_ways, i_slots, i_sums, 0, 0, EARLY, 48, 32, 64, i_inbox, 0)
    X = Part("X", links, i_ways, i_slots, i_sums, 8 * EARLY, EARLY, LATE, 32, 16, 64, i_inbox, 8 * EARLY)
    T = Part("T", links, t_ways, t_slots, t_slots, 0, 0, FIRST, 32, 16, 48, t_inbox, 0)
    U = Part("U", links, t_ways, t_slots, t_slots, 16 * FIRST, FIRST, FIRST, 32, 16, 48, t_inbox, 8 * FIRST)
    V = Part("V", links, t_ways, t_slots, t_slots, 32 * FIRST, 2 * FIRST, LAST, 16, 16, 32, t_inbox, 16 * FIRST)

    def pairs(part, sibs, r, n):
        return pl.ds(part.base + ((4 * sibs + r) * 2) * part.rows, 2 * n * part.rows)

    def sib_rows(part, r, n):
        return pl.ds(part.base // 2 + r * 2 * part.rows, 2 * n * part.rows)

    def to_sibling(part, *rs):
        for r in rs:
            src, dst = pairs(part, 0, r, 1), pairs(part, 1, r, 1)
            links.send(f"{part.tag}to{r}", lambda src=src: t_slots.at[src], lambda dst=dst: t_slots.at[dst], sibling)

    def crossed(part, *rs):
        links.arrived(*(f"{part.tag}to{r}" for r in rs))

    for part in (Y, X, T, U, V):
        part.plan_gather()
        part.plan_sums()
    for part in (T, U, V):
        for r in (2, 0):
            src, dst = pairs(part, 1, r, 2), sib_rows(part, r, 2)
            links.plan(f"{part.tag}back{r}", lambda src=src: t_slots.at[src], lambda dst=dst: t_sib.at[dst], sibling)

    def back_to_sibling(part):
        for r in (2, 0):
            links.start(f"{part.tag}back{r}")

    def from_sibling(part, r):
        links.arrived(f"{part.tag}back{r}")
        mine = dt[pairs(part, 0, r, 2), :] + t_sib[sib_rows(part, r, 2), :].astype(f32)
        if r == 0:
            t_own[pl.ds(part.first, part.rows), :] = mine[: part.rows]
        t_slots[pairs(part, 0, r, 2), :] = mine.astype(bf16)

    factor, bias = scale_ref[0], bias_ref[0]

    def nothing():
        pass

    def products(text_parts, image_part, first_t, first_i, hooks):
        tn, n, turns = 16 * text_parts[0].rows, 8 * image_part.rows, len(text_parts)
        i_at = pl.ds(image_part.base, n)

        def step(k):
            def at_step(calls):
                for turn in range(turns):
                    if calls[turn] is not nothing:
                        calls[turn]() if turns == 1 else pl.when(k == turn)(calls[turn])

            t0 = text_parts[0].base + k * tn
            t0 = t0 if turns == 1 else pl.multiple_of(t0, 128)
            t_at = pl.ds(t0, tn)
            logits = factor * dot(t_slots[t_at, :], i_slots[i_at, :], 1, 1) + bias
            e = jnp.exp(-logits)
            w = 1.0 / (1.0 + e)
            here = where_ref[:, i_at] - t0 == lax.broadcasted_iota(jnp.int32, (tn, n), 0)
            w_ref[pl.ds(0, tn), pl.ds(0, n)] = jnp.where(here, -e * w, w).astype(bf16)
            at_step(hooks[0])
            g = dot(w_ref[pl.ds(0, tn), pl.ds(0, n)], t_slots[t_at, :], 0, 0)
            if not first_i:
                di[i_at, :] += g
            elif turns == 1:
                di[i_at, :] = g
            else:
                di[i_at, :] = jnp.where(k == 0, g, di[i_at, :] + g)
            at_step(hooks[1])
            d = dot(w_ref[pl.ds(0, tn), pl.ds(0, n)], i_slots[i_at, :], 1, 0)
            if first_t:
                dt[t_at, :] = d
            else:
                d = dt[t_at, :] + d
                dt[pl.ds(t0, tn // 2), :] = d[: tn // 2]
                theirs = t0 + tn // 2
                t_slots[pl.ds(theirs if turns == 1 else pl.multiple_of(theirs, 128), tn // 2), :] = d[tn // 2 :].astype(bf16)
            at_step(hooks[2])

        if turns == 1:
            step(0)
        else:
            pl.loop(0, turns)(step)

    def ready(part, *rs):
        for r in rs:
            where = part.span(r, 0, (0, 2 * part.rows))
            i_sums[where, :] = di[where, :].astype(bf16)

    def each(name, *parts):
        for part in parts:
            getattr(part, name)()

    def steps(*calls):
        def run():
            for call, *args in calls:
                call(*args)

        return run

    each("gather_start", Y, T)
    lane = lax.broadcasted_iota(jnp.int32, (1, IMAGES), 1)
    is_late = lane >= 8 * EARLY
    inner = jnp.where(is_late, lane - 8 * EARLY, lane)
    slot_of = jnp.where(is_late, floor_div(inner, LATE), floor_div(inner, EARLY))
    row_of = inner - slot_of * jnp.where(is_late, LATE, EARLY) + jnp.where(is_late, EARLY, 0)
    pick = (lax.broadcasted_iota(jnp.int32, (ROWS, IMAGES), 0) == row_of).astype(bf16)
    high, low = matches[...] >> 8, matches[...] & 255
    high, low = dot(high.astype(f32).astype(bf16), pick, 1, 0), dot(low.astype(f32).astype(bf16), pick, 1, 0)
    m_slots[0] = high.astype(jnp.int32) * 256 + low.astype(jnp.int32)
    for r in range(4):
        for p in range(2):
            if (r, p) != (0, 0):
                k = ((4 - r) % 4) * 2 + p
                links.send(f"m{k}", lambda: m_slots.at[0], lambda k=k: m_slots.at[k], peers[r, p])
    each("gather_pair", T, Y)
    each("gather_a", T, Y)
    each("gather_b", T, Y)
    U.gather_start()
    T.arrived("gA")
    to_sibling(T, 0)
    each("gather_a2", T, Y)
    each("gather_c", T, Y)
    X.gather_start()
    links.arrived(*(f"m{k}" for k in range(1, 8)))
    match = m_slots[0]
    for k in range(1, 8):
        match = jnp.where(slot_of == k, m_slots[k], match)
    owner = floor_div(match, ROWS)
    row = match - owner * ROWS
    b, g = owner >> 3, owner & 7
    ox = ((b >> 1) & 1) * 2 + (g & 1)
    held = ((g >> 1) == y) & ((ox == x) | (ox == xt))
    slot = jnp.where((b & 1) == core, 0, 8) + (((b >> 2) - z + 4) & 3) * 2 + jnp.where(ox == x, 0, 1)
    spot = jnp.where(row < FIRST, slot * FIRST + row, 16 * FIRST + slot * FIRST + row - FIRST)
    spot = jnp.where(row < 2 * FIRST, spot, 32 * FIRST + slot * LAST + row - 2 * FIRST)
    where_ref[...] = jnp.where(held, spot, -1)

    T.arrived("gD1", "gD3")
    to_sibling(T, 1, 3)
    each("gather_pair", U)
    T.arrived("gB20", "gB21", "gC20", "gC21", "gD2")
    to_sibling(T, 2)
    each("gather_a", U)
    each("gather_b", U)
    V.gather_start()
    Y.arrived("gB20", "gB21", "gC20", "gC21", "gD2", "gA", "gD1", "gD3")
    crossed(T, 0, 1, 3, 2)

    def finish_texts(part):
        rows = pl.ds(part.first, part.rows)
        total = part.total(t_own[rows, :])
        text_grad[rows, :] = norm_back(texts[rows, :], factor * total)

    def finish_images(part):
        rows = pl.ds(part.first, part.rows)
        total = part.total(di[pl.ds(part.base, part.rows), :])
        image_grad[rows, :] = norm_back(images[rows, :], factor * total)

    products((T, U), Y, True, True, (
        (
            steps((each, "gather_a2", U), (each, "gather_c", U), (each, "gather_pair", X)),
            steps((each, "gather_a2", X, V), (each, "gather_c", X, V)),
        ),
        (
            steps(
                (U.arrived, "gA", "gD1", "gD3"), (to_sibling, U, 0, 1, 3),
                (U.arrived, "gB20", "gB21", "gC20", "gC21", "gD2"), (to_sibling, U, 2),
                (each, "gather_a", X), (each, "gather_b", X),
                (each, "gather_pair", V), (each, "gather_a", V), (each, "gather_b", V),
            ),
            steps(
                (V.arrived, "gA", "gD1", "gD3"), (to_sibling, V, 0, 1, 3),
                (V.arrived, "gB20", "gB21", "gC20", "gC21", "gD2"), (to_sibling, V, 2),
            ),
        ),
        (steps((crossed, U, 0, 1, 3, 2)), nothing),
    ))
    crossed(V, 0, 1, 3, 2)
    links.finish()
    products((V,), Y, True, False, (
        (nothing,),
        (steps((ready, Y, 2), (Y.sum_far,), (ready, Y, 1, 3, 0), (Y.sum_pair, 1), (Y.sum_pair, 3), (Y.sum_pair, 0)),),
        (nothing,),
    ))
    X.arrived("gB20", "gB21", "gC20", "gC21", "gD2", "gA", "gD1", "gD3")
    products((T, U), X, False, True, (
        (nothing, steps((Y.sum_near_a, 1), (Y.sum_near_a, 3))),
        (
            steps((Y.sum_far_a,), (Y.sum_near, 1), (Y.sum_near, 3)),
            steps(
                (from_sibling, T, 2), (T.sum_far,), (from_sibling, T, 0), *((T.sum_pair, r) for r in (1, 3, 0)),
                (Y.sum_own_b,),
            ),
        ),
        (steps((back_to_sibling, T)), steps((back_to_sibling, U))),
    ))
    products((V,), X, False, False, (
        (steps((T.sum_far_a,), (T.sum_near, 1), (T.sum_near, 3)),),
        (steps(
            (ready, X, 2), (X.sum_far,), (ready, X, 1, 3, 0), *((X.sum_pair, r) for r in (1, 3, 0)),
            (from_sibling, U, 2), (U.sum_far,), (from_sibling, U, 0), *((U.sum_pair, r) for r in (1, 3, 0)),
            (T.sum_near_a, 1), (T.sum_near_a, 3),
        ),),
        (steps((back_to_sibling, V), (finish_images, Y)),),
    ))
    T.sum_own_b()
    X.sum_far_a()
    U.sum_far_a()
    for part in (X, U):
        part.sum_near(1)
        part.sum_near(3)
    from_sibling(V, 2)
    V.sum_far()
    from_sibling(V, 0)
    for r in (1, 3, 0):
        V.sum_pair(r)
    for part in (X, U):
        part.sum_near_a(1)
        part.sum_near_a(3)
    V.sum_far_a()
    V.sum_near(1)
    V.sum_near(3)
    finish_texts(T)
    U.sum_own_b()
    V.sum_near_a(1)
    V.sum_near_a(3)
    X.sum_own_b()
    finish_texts(U)
    V.sum_own_b()
    finish_images(X)
    finish_texts(V)
    links.finish()


def per_device(images, texts, match, logit_scale, logit_bias):
    vmem = pl.BlockSpec(memory_space=pltpu.VMEM)
    smem = pl.BlockSpec(memory_space=pltpu.SMEM)
    rows = lambda n: pltpu.VMEM((n, WIDTH), bf16)
    return pl.pallas_call(
        kernel,
        out_shape=(jax.ShapeDtypeStruct((ROWS, WIDTH), f32), jax.ShapeDtypeStruct((ROWS, WIDTH), f32)),
        in_specs=[vmem, vmem, vmem, smem, smem],
        out_specs=(vmem, vmem),
        scratch_shapes=[
            rows(IMAGES), rows(TEXTS), pltpu.VMEM((8, 1, IMAGES), jnp.int32), pltpu.VMEM((1, IMAGES), jnp.int32),
            pltpu.VMEM((16 * FIRST, 8 * EARLY), bf16), pltpu.VMEM((IMAGES, WIDTH), f32), pltpu.VMEM((TEXTS, WIDTH), f32),
            pltpu.VMEM((ROWS, WIDTH), f32), rows(IMAGES), rows(IMAGES), rows(IMAGES), rows(IMAGES),
            pltpu.SemaphoreType.DMA((SEMS,)), pltpu.SemaphoreType.DMA((SEMS,)),
        ],
        compiler_params=pltpu.CompilerParams(collective_id=0, has_side_effects=True, vmem_limit_bytes=62 << 20),
        cost_estimate=pl.CostEstimate(
            flops=6 * IMAGES * TEXTS * WIDTH, bytes_accessed=8 * ROWS * WIDTH, transcendentals=2 * IMAGES * TEXTS
        ),
        name="contrastive",
    )(images, texts, match[None, :], logit_scale, logit_bias)


def solution(mesh):
    rows = P(("blk", "group"), None)
    return jax.shard_map(
        per_device,
        mesh=mesh,
        in_specs=(rows, rows, P(("blk", "group")), P(), P()),
        out_specs=(rows, rows),
        check_vma=False,
    )
```

profile of v0, /device:TPU:0, one launch (start us, length us, event | category | flops | bytes accessed | tf_op | source)
XLA Modules:
  0.0 103.3 jit_solution(4767249442667331392)
XLA Ops:
  1.9 98.3 %contrastive.1 = (f32[176,1152]{1,0:T(8,128)}, f32[176,1152]{1,0:T(8,128)}) custom-call(bf16[176,1152]{1,0:T(8,128)(2,1)} %images.1, bf16[176,1152]{1,0:T(8,128)(2,1)} %texts.1, s32[1,176]{1,0:T(1,128)} %bitcast.1, f32[1]{0:T(128)S(6)} %copy.9.scale_ref, f32[1]{0:T(128)S(6)} %copy.10.bias_ref), custom_call_target="tpu_custom_call" | custom-call | flops 27405582336 | bytes 1622016 | tf_op jit(solution)/shard_map/contrastive/pallas_call | solution.py:473
  100.2 0.0 copy-start
  100.3 2.2 %copy.11 = f32[176,1152]{1,0:T(8,128)} copy(f32[176,1152]{1,0:T(8,128)} %get-tuple-element.4) | data formatting | bytes 1622016
  102.4 0.0 copy-done
  102.4 0.9 copy.12
Async XLA Ops:
  100.2 2.2 %copy-start = (f32[176,1152]{1,0:T(8,128)S(1)}, f32[176,1152]{1,0:T(8,128)}, u32[]{:S(2)}) copy-start(f32[176,1152]{1,0:T(8,128)} %get-tuple-element.5) | copy-start | bytes 2433028
where the time goes:
time: 103 us
  Pallas kernels  98.3 us (95%)
  local copies, waits for them, and re-layouts  3.05 us (3%)
  between operations  1.94 us (2%)
    pallas_call x1, Pallas kernels, per_device(): pl.pallas_call(kernel, out_shape=(jax.ShapeDtypeStruct((ROWS, WIDTH), f32...  98.3 us
    unnamed x4, local copies, waits for them, and re-layouts  3.05 us

commit v1 on v0

--- a/solution.py
+++ b/solution.py
@@ -8,7 +8,7 @@
 epsilon = 1e-06
 MESH = pl.DeviceIdType.MESH
 ROWS, WIDTH = 176, 1152
-EARLY, LATE = 96, 80
+EARLY, LATE = 80, 96
 FIRST, LAST = 64, 48
 IMAGES, TEXTS = 8 * ROWS, 16 * ROWS
 SEMS = 208
@@ -76,7 +76,8 @@
         self.up, self.down, self.partner = ways
         self.slots, self.sums, self.base, self.first, self.rows = slots, sums, base, first, rows
         self.all, self.a, self.b = (0, rows), (0, cut), (cut, rows)
-        self.a0, self.a1, self.b0, self.b1 = (0, half_a), (half_a, cut), (cut, half_b), (half_b, rows)
+        self.a0, self.a1 = (0, half_a), (half_a, cut)
+        self.halves = tuple(((cut, at), (at, rows)) for at in (half_b, cut + rows - half_b))
         self.inbox, self.box, self.boxes, self.empty = inbox, box, {}, set()
 
     def span(self, r, p, part):
@@ -105,7 +106,7 @@
         moves += [(f"gD{r}", r, 0, r, 1, a, partner) for r in (1, 2, 3)]
         for name, p, part in (("gA", 0, a), ("gB", 0, b), ("gC", 1, b)):
             moves += [(name + "3", 0, p, 3, p, part, up), (name + "1", 0, p, 1, p, part, down)]
-            half0, half1 = (self.a0, self.a1) if part is a else (self.b0, self.b1)
+            half0, half1 = (self.a0, self.a1) if part is a else self.halves[p]
             moves += [(name + "20", 1, p, 2, p, half0, down), (name + "21", 3, p, 2, p, half1, up)]
         for name, r, p, to_r, to_p, part, target in moves:
             self.plan(name, part, self.at(r, p, part), self.at(to_r, to_p, part), target)
@@ -139,7 +140,7 @@
         moves += [("sHA1", 2, 0, self.a0, up), ("sHA3", 2, 0, self.a1, down)]
         moves += [("sRA1", 1, 0, self.a, up), ("sRA3", 3, 0, self.a, down)]
         for p in (0, 1):
-            moves += [(f"sH1{p}", 2, p, self.b0, up), (f"sH3{p}", 2, p, self.b1, down)]
+            moves += [(f"sH1{p}", 2, p, self.halves[p][0], up), (f"sH3{p}", 2, p, self.halves[p][1], down)]
             moves += [(f"sR1{p}", 1, p, self.b, up), (f"sR3{p}", 3, p, self.b, down)]
         for name, r, p, part, target in moves:
             src, size = self.span(r, p, part), part[1] - part[0]
@@ -171,9 +172,8 @@
         self.give(f"sX{r}")
 
     def sum_near(self, r):
-        half = self.b0 if r == 1 else self.b1
         for p in (1, 0):
-            self.add(r, p, half, f"sH{r}{p}")
+            self.add(r, p, self.halves[p][r // 2], f"sH{r}{p}")
             self.give(f"sR{r}{p}")
 
     def sum_near_a(self, r):
@@ -202,7 +202,7 @@
 
 def kernel(
     images, texts, matches, scale_ref, bias_ref, image_grad, text_grad,
-    i_slots, t_slots, m_slots, where_ref, w_ref, di, dt, t_own, t_sib, i_sums, i_inbox, t_inbox, send_sems, recv_sems,
+    i_slots, t_slots, m_slots, where_ref, w_ref, di, dt, t_own, t_out, t_sib, i_sums, i_inbox, t_inbox, send_sems, recv_sems,
 ):
     x, y, z, core = place()
     odd = lax.rem(x, 2)
@@ -229,8 +229,8 @@
     pl.semaphore_wait(barrier, len(greeted))
 
     links = Links(send_sems, recv_sems)
-    Y = Part("Y", links, i_ways, i_slots, i_sums, 0, 0, EARLY, 48, 32, 64, i_inbox, 0)
-    X = Part("X", links, i_ways, i_slots, i_sums, 8 * EARLY, EARLY, LATE, 32, 16, 64, i_inbox, 8 * EARLY)
+    Y = Part("Y", links, i_ways, i_slots, i_sums, 0, 0, EARLY, 32, 16, 64, i_inbox, 0)
+    X = Part("X", links, i_ways, i_slots, i_sums, 8 * EARLY, EARLY, LATE, 48, 32, 64, i_inbox, 8 * EARLY)
     T = Part("T", links, t_ways, t_slots, t_slots, 0, 0, FIRST, 32, 16, 48, t_inbox, 0)
     U = Part("U", links, t_ways, t_slots, t_slots, 16 * FIRST, FIRST, FIRST, 32, 16, 48, t_inbox, 8 * FIRST)
     V = Part("V", links, t_ways, t_slots, t_slots, 32 * FIRST, 2 * FIRST, LAST, 16, 16, 32, t_inbox, 16 * FIRST)
@@ -254,8 +254,10 @@
         part.plan_sums()
     for part in (T, U, V):
         for r in (2, 0):
-            src, dst = pairs(part, 1, r, 2), sib_rows(part, r, 2)
-            links.plan(f"{part.tag}back{r}", lambda src=src: t_slots.at[src], lambda dst=dst: t_sib.at[dst], sibling)
+            where = sib_rows(part, r, 2)
+            links.plan(
+                f"{part.tag}back{r}", lambda where=where: t_out.at[where], lambda where=where: t_sib.at[where], sibling
+            )
 
     def back_to_sibling(part):
         for r in (2, 0):
@@ -273,9 +275,28 @@
     def nothing():
         pass
 
-    def products(text_parts, image_part, first_t, first_i, hooks):
+    def products(text_parts, image_part, first_t, first_i, hooks, texts_first=False):
         tn, n, turns = 16 * text_parts[0].rows, 8 * image_part.rows, len(text_parts)
         i_at = pl.ds(image_part.base, n)
+
+        def image_grads(k, t0):
+            g = dot(w_ref[pl.ds(0, tn), pl.ds(0, n)], t_slots[pl.ds(t0, tn), :], 0, 0)
+            if not first_i:
+                di[i_at, :] += g
+            elif turns == 1:
+                di[i_at, :] = g
+            else:
+                di[i_at, :] = jnp.where(k == 0, g, di[i_at, :] + g)
+
+        def text_grads(k, t0):
+            d = dot(w_ref[pl.ds(0, tn), pl.ds(0, n)], i_slots[i_at, :], 1, 0)
+            if first_t:
+                dt[pl.ds(t0, tn), :] = d
+            else:
+                d = dt[pl.ds(t0, tn), :] + d
+                dt[pl.ds(t0, tn // 2), :] = d[: tn // 2]
+                out = t0 // 2 if turns == 1 else pl.multiple_of(text_parts[0].base // 2 + k * (tn // 2), 128)
+                t_out[pl.ds(out, tn // 2), :] = d[tn // 2 :].astype(bf16)
 
         def step(k):
             def at_step(calls):
@@ -292,22 +313,10 @@
             here = where_ref[:, i_at] - t0 == lax.broadcasted_iota(jnp.int32, (tn, n), 0)
             w_ref[pl.ds(0, tn), pl.ds(0, n)] = jnp.where(here, -e * w, w).astype(bf16)
             at_step(hooks[0])
-            g = dot(w_ref[pl.ds(0, tn), pl.ds(0, n)], t_slots[t_at, :], 0, 0)
-            if not first_i:
-                di[i_at, :] += g
-            elif turns == 1:
-                di[i_at, :] = g
-            else:
-                di[i_at, :] = jnp.where(k == 0, g, di[i_at, :] + g)
+            order = (text_grads, image_grads) if texts_first else (image_grads, text_grads)
+            order[0](k, t0)
             at_step(hooks[1])
-            d = dot(w_ref[pl.ds(0, tn), pl.ds(0, n)], i_slots[i_at, :], 1, 0)
-            if first_t:
-                dt[t_at, :] = d
-            else:
-                d = dt[t_at, :] + d
-                dt[pl.ds(t0, tn // 2), :] = d[: tn // 2]
-                theirs = t0 + tn // 2
-                t_slots[pl.ds(theirs if turns == 1 else pl.multiple_of(theirs, 128), tn // 2), :] = d[tn // 2 :].astype(bf16)
+            order[1](k, t0)
             at_step(hooks[2])
 
         if turns == 1:
@@ -418,31 +427,33 @@
     ))
     X.arrived("gB20", "gB21", "gC20", "gC21", "gD2", "gA", "gD1", "gD3")
     products((T, U), X, False, True, (
-        (nothing, steps((Y.sum_near_a, 1), (Y.sum_near_a, 3))),
         (
-            steps((Y.sum_far_a,), (Y.sum_near, 1), (Y.sum_near, 3)),
+            nothing,
             steps(
                 (from_sibling, T, 2), (T.sum_far,), (from_sibling, T, 0), *((T.sum_pair, r) for r in (1, 3, 0)),
-                (Y.sum_own_b,),
+                (Y.sum_near_a, 1), (Y.sum_near_a, 3),
             ),
         ),
-        (steps((back_to_sibling, T)), steps((back_to_sibling, U))),
-    ))
+        (
+            steps((back_to_sibling, T), (Y.sum_far_a,), (Y.sum_near, 1), (Y.sum_near, 3)),
+            steps((back_to_sibling, U), (T.sum_far_a,), (T.sum_near, 1), (T.sum_near, 3)),
+        ),
+        (nothing, steps((T.sum_near_a, 1), (T.sum_near_a, 3), (Y.sum_own_b,))),
+    ), texts_first=True)
     products((V,), X, False, False, (
-        (steps((T.sum_far_a,), (T.sum_near, 1), (T.sum_near, 3)),),
+        (steps(
+            (from_sibling, U, 2), (U.sum_far,), (from_sibling, U, 0), *((U.sum_pair, r) for r in (1, 3, 0)),
+        ),),
         (steps(
             (ready, X, 2), (X.sum_far,), (ready, X, 1, 3, 0), *((X.sum_pair, r) for r in (1, 3, 0)),
-            (from_sibling, U, 2), (U.sum_far,), (from_sibling, U, 0), *((U.sum_pair, r) for r in (1, 3, 0)),
-            (T.sum_near_a, 1), (T.sum_near_a, 3),
+            (U.sum_far_a,), (U.sum_near, 1), (U.sum_near, 3),
         ),),
         (steps((back_to_sibling, V), (finish_images, Y)),),
     ))
     T.sum_own_b()
     X.sum_far_a()
-    U.sum_far_a()
-    for part in (X, U):
-        part.sum_near(1)
-        part.sum_near(3)
+    X.sum_near(1)
+    X.sum_near(3)
     from_sibling(V, 2)
     V.sum_far()
     from_sibling(V, 0)
@@ -472,16 +483,16 @@
     rows = lambda n: pltpu.VMEM((n, WIDTH), bf16)
     return pl.pallas_call(
         kernel,
-        out_shape=(jax.ShapeDtypeStruct((ROWS, WIDTH), f32), jax.ShapeDtypeStruct((ROWS, WIDTH), f32)),
+        out_shape=(pltpu.VMEM((ROWS, WIDTH), f32), pltpu.VMEM((ROWS, WIDTH), f32)),
         in_specs=[vmem, vmem, vmem, smem, smem],
         out_specs=(vmem, vmem),
         scratch_shapes=[
             rows(IMAGES), rows(TEXTS), pltpu.VMEM((8, 1, IMAGES), jnp.int32), pltpu.VMEM((1, IMAGES), jnp.int32),
-            pltpu.VMEM((16 * FIRST, 8 * EARLY), bf16), pltpu.VMEM((IMAGES, WIDTH), f32), pltpu.VMEM((TEXTS, WIDTH), f32),
-            pltpu.VMEM((ROWS, WIDTH), f32), rows(IMAGES), rows(IMAGES), rows(IMAGES), rows(IMAGES),
+            pltpu.VMEM((16 * FIRST, 8 * LATE), bf16), pltpu.VMEM((IMAGES, WIDTH), f32), pltpu.VMEM((TEXTS, WIDTH), f32),
+            pltpu.VMEM((ROWS, WIDTH), f32), rows(IMAGES), rows(IMAGES), rows(IMAGES), rows(IMAGES), rows(IMAGES),
             pltpu.SemaphoreType.DMA((SEMS,)), pltpu.SemaphoreType.DMA((SEMS,)),
         ],
-        compiler_params=pltpu.CompilerParams(collective_id=0, has_side_effects=True, vmem_limit_bytes=62 << 20),
+        compiler_params=pltpu.CompilerParams(collective_id=0, has_side_effects=True, vmem_limit_bytes=60 << 20),
         cost_estimate=pl.CostEstimate(
             flops=6 * IMAGES * TEXTS * WIDTH, bytes_accessed=8 * ROWS * WIDTH, transcendentals=2 * IMAGES * TEXTS
         ),

time: 103 us -> 99.9 us (0.970)
  Pallas kernels: 98.3 us -> 96.1 us
  local copies, waits for them, and re-layouts: 3.05 us -> 1.78 us
    pallas_call x1, Pallas kernels: 98.3 us -> 96.1 us  [per_device(): pl.pallas_call(kernel, out_shape=(pltpu.VMEM((ROWS, WIDTH), f32), pltpu.V...]
    unnamed x4 -> x2, local copies, waits for them, and re-layouts: 3.05 us -> 1.78 us
where the time goes in v1:
time: 99.9 us; the launch traced here: 99.8 us
  Pallas kernels  96.1 us (96%)
  between operations  1.93 us (2%)
  local copies, waits for them, and re-layouts  1.78 us (2%)
    pallas_call x1, Pallas kernels, per_device(): pl.pallas_call(kernel, out_shape=(pltpu.VMEM((ROWS, WIDTH), f32), pltpu.V...  96.1 us

profile of v1, /device:TPU:0, one launch (start us, length us, event | category | flops | bytes accessed | tf_op | source)
XLA Modules:
  0.0 99.8 jit_solution(15600650470070699817)
XLA Ops:
  1.9 96.1 %contrastive.1 = (f32[176,1152]{1,0:T(8,128)S(1)}, f32[176,1152]{1,0:T(8,128)S(1)}) custom-call(bf16[176,1152]{1,0:T(8,128)(2,1)} %images.1, bf16[176,1152]{1,0:T(8,128)(2,1)} %texts.1, s32[1,176]{1,0:T(1,128)} %bitcast.1, f32[1]{0:T(128)S(6)} %copy.11.scale_ref, f32[1]{0:T(128)S(6)} %copy.12.bias_ref), custom_call_target="tpu_custom_call" | custom-call | flops 27405582336 | bytes 1622016 | tf_op jit(solution)/shard_map/contrastive/pallas_call | solution.py:484
  98.0 0.9 copy.9
  98.9 0.9 copy.10

commit v2 on v1

--- a/solution.py
+++ b/solution.py
@@ -444,34 +444,29 @@
         (steps(
             (from_sibling, U, 2), (U.sum_far,), (from_sibling, U, 0), *((U.sum_pair, r) for r in (1, 3, 0)),
         ),),
+        (steps((back_to_sibling, V), (U.sum_far_a,), (U.sum_near, 1), (U.sum_near, 3)),),
         (steps(
             (ready, X, 2), (X.sum_far,), (ready, X, 1, 3, 0), *((X.sum_pair, r) for r in (1, 3, 0)),
-            (U.sum_far_a,), (U.sum_near, 1), (U.sum_near, 3),
+            (T.sum_own_b,), (from_sibling, V, 2), (V.sum_far,), (from_sibling, V, 0),
+            *((V.sum_pair, r) for r in (1, 3, 0)), (U.sum_near_a, 1), (U.sum_near_a, 3),
         ),),
-        (steps((back_to_sibling, V), (finish_images, Y)),),
-    ))
-    T.sum_own_b()
+    ), texts_first=True)
     X.sum_far_a()
     X.sum_near(1)
     X.sum_near(3)
-    from_sibling(V, 2)
-    V.sum_far()
-    from_sibling(V, 0)
-    for r in (1, 3, 0):
-        V.sum_pair(r)
-    for part in (X, U):
-        part.sum_near_a(1)
-        part.sum_near_a(3)
     V.sum_far_a()
     V.sum_near(1)
     V.sum_near(3)
+    U.sum_own_b()
+    finish_images(Y)
+    X.sum_near_a(1)
+    X.sum_near_a(3)
     finish_texts(T)
-    U.sum_own_b()
     V.sum_near_a(1)
     V.sum_near_a(3)
     X.sum_own_b()
+    V.sum_own_b()
     finish_texts(U)
-    V.sum_own_b()
     finish_images(X)
     finish_texts(V)
     links.finish()

time: 99.9 us -> 98.5 us (0.986)
  Pallas kernels: 96.1 us -> 94.6 us
    pallas_call x1, Pallas kernels: 96.1 us -> 94.6 us  [per_device(): pl.pallas_call(kernel, out_shape=(pltpu.VMEM((ROWS, WIDTH), f32), pltpu.V...]
where the time goes in v2:
time: 98.5 us; the launch traced here: 98.3 us
  Pallas kernels  94.6 us (96%)
  between operations  1.93 us (2%)
  local copies, waits for them, and re-layouts  1.78 us (2%)
    pallas_call x1, Pallas kernels, per_device(): pl.pallas_call(kernel, out_shape=(pltpu.VMEM((ROWS, WIDTH), f32), pltpu.V...  94.6 us

profile of v2, /device:TPU:0, one launch (start us, length us, event | category | flops | bytes accessed | tf_op | source)
XLA Modules:
  0.0 98.3 jit_solution(9972187608561968374)
XLA Ops:
  1.9 94.6 %contrastive.1 = (f32[176,1152]{1,0:T(8,128)S(1)}, f32[176,1152]{1,0:T(8,128)S(1)}) custom-call(bf16[176,1152]{1,0:T(8,128)(2,1)} %images.1, bf16[176,1152]{1,0:T(8,128)(2,1)} %texts.1, s32[1,176]{1,0:T(1,128)} %bitcast.1, f32[1]{0:T(128)S(6)} %copy.11.scale_ref, f32[1]{0:T(128)S(6)} %copy.12.bias_ref), custom_call_target="tpu_custom_call" | custom-call | flops 27405582336 | bytes 1622016 | tf_op jit(solution)/shard_map/contrastive/pallas_call | solution.py:479
  96.6 0.9 copy.9
  97.5 0.9 copy.10

commit v3 on v2

--- a/solution.py
+++ b/solution.py
@@ -8,7 +8,7 @@
 epsilon = 1e-06
 MESH = pl.DeviceIdType.MESH
 ROWS, WIDTH = 176, 1152
-EARLY, LATE = 80, 96
+EARLY, LATE = 96, 80
 FIRST, LAST = 64, 48
 IMAGES, TEXTS = 8 * ROWS, 16 * ROWS
 SEMS = 208
@@ -229,8 +229,8 @@
     pl.semaphore_wait(barrier, len(greeted))
 
     links = Links(send_sems, recv_sems)
-    Y = Part("Y", links, i_ways, i_slots, i_sums, 0, 0, EARLY, 32, 16, 64, i_inbox, 0)
-    X = Part("X", links, i_ways, i_slots, i_sums, 8 * EARLY, EARLY, LATE, 48, 32, 64, i_inbox, 8 * EARLY)
+    Y = Part("Y", links, i_ways, i_slots, i_sums, 0, 0, EARLY, 48, 32, 64, i_inbox, 0)
+    X = Part("X", links, i_ways, i_slots, i_sums, 8 * EARLY, EARLY, LATE, 32, 16, 64, i_inbox, 8 * EARLY)
     T = Part("T", links, t_ways, t_slots, t_slots, 0, 0, FIRST, 32, 16, 48, t_inbox, 0)
     U = Part("U", links, t_ways, t_slots, t_slots, 16 * FIRST, FIRST, FIRST, 32, 16, 48, t_inbox, 8 * FIRST)
     V = Part("V", links, t_ways, t_slots, t_slots, 32 * FIRST, 2 * FIRST, LAST, 16, 16, 32, t_inbox, 16 * FIRST)
@@ -483,7 +483,7 @@
         out_specs=(vmem, vmem),
         scratch_shapes=[
             rows(IMAGES), rows(TEXTS), pltpu.VMEM((8, 1, IMAGES), jnp.int32), pltpu.VMEM((1, IMAGES), jnp.int32),
-            pltpu.VMEM((16 * FIRST, 8 * LATE), bf16), pltpu.VMEM((IMAGES, WIDTH), f32), pltpu.VMEM((TEXTS, WIDTH), f32),
+            pltpu.VMEM((16 * FIRST, 8 * EARLY), bf16), pltpu.VMEM((IMAGES, WIDTH), f32), pltpu.VMEM((TEXTS, WIDTH), f32),
             pltpu.VMEM((ROWS, WIDTH), f32), rows(IMAGES), rows(IMAGES), rows(IMAGES), rows(IMAGES), rows(IMAGES),
             pltpu.SemaphoreType.DMA((SEMS,)), pltpu.SemaphoreType.DMA((SEMS,)),
         ],

time: 98.5 us -> 99.2 us (level)
  no operation moved by 1% of the time
where the time goes in v3:
time: 99.2 us; the launch traced here: 99.1 us
  Pallas kernels  95.3 us (96%)
  between operations  1.93 us (2%)
  local copies, waits for them, and re-layouts  1.78 us (2%)
    pallas_call x1, Pallas kernels, per_device(): pl.pallas_call(kernel, out_shape=(pltpu.VMEM((ROWS, WIDTH), f32), pltpu.V...  95.3 us

profile of v3, /device:TPU:0, one launch (start us, length us, event | category | flops | bytes accessed | tf_op | source)
XLA Modules:
  0.0 99.1 jit_solution(6472980470632776432)
XLA Ops:
  1.9 95.3 %contrastive.1 = (f32[176,1152]{1,0:T(8,128)S(1)}, f32[176,1152]{1,0:T(8,128)S(1)}) custom-call(bf16[176,1152]{1,0:T(8,128)(2,1)} %images.1, bf16[176,1152]{1,0:T(8,128)(2,1)} %texts.1, s32[1,176]{1,0:T(1,128)} %bitcast.1, f32[1]{0:T(128)S(6)} %copy.11.scale_ref, f32[1]{0:T(128)S(6)} %copy.12.bias_ref), custom_call_target="tpu_custom_call" | custom-call | flops 27405582336 | bytes 1622016 | tf_op jit(solution)/shard_map/contrastive/pallas_call | solution.py:479
  97.3 0.9 copy.9
  98.2 0.9 copy.10
